TPU v7x, 32 devices: a whole 2x2x4 slice. The times are simulated.
32 devices in a mesh: groups: 2 (over y), adapter: 4 (over x, core), tensor: 4 (over z).
Axes of the slice: x: 2, y: 2, z: 4, core: 2. Of those that a mesh axis runs over, the one named last changes fastest.
Arguments:
- hidden: bfloat16 [1024, 28672], P(('groups', 'adapter'), 'tensor'), parts along dimension 0, may hold values from -6 to 6
- base_down_weight: bfloat16 [28672, 8192], P('tensor', 'adapter'), may hold values from -0.03125 to 0.03125
- adapter_input_factors: bfloat16 [32, 28672, 64], P('adapter', 'tensor'), may hold values from -0.03125 to 0.03125
- adapter_output_factors: bfloat16 [32, 64, 8192], P(None, 'tensor', 'adapter'), may hold values from -0.75 to 0.75
- adapter_of_request: int32 [1024, 1], P('groups'), parts along dimension 0, may hold values from 0 to 31; in each aligned block of 128 rows (0 to 127, 128 to 255, ...) at most 4 rows name the same one
Outputs:
- mixed: bfloat16 [1024, 8192], P(('groups', 'tensor'), 'adapter'), parts along dimension 0
There are 2 independent parts, one for each index of `groups`. A program takes and returns all parts, laid end to end along the dimension named above; an argument that names none is the same for every part. Nothing has to cross between parts.
Inputs may be any that keep to these rules, and one draw needn't show every extreme that they name: `adapter_of_request`: in each aligned block of 128 rows no adapter is named by more than 4 rows, a bound that some block reaches.
All inputs are finite; a program needn't handle non-finite values.
Results may differ from a plain program's by a relative error of at most 0.0039.
Values may be sent and summed in bfloat16 or wider, within the bound.
A program may use at most 128 MiB of HBM per device.

v0:
```python
import jax
import jax.numpy as jnp
from jax import lax
from jax.sharding import PartitionSpec as P

MOST = 4


def slot_numbers(flat_ids, blocks, block_rows):
    grouped = flat_ids.reshape(blocks, block_rows)
    matches = grouped[:, :, None] == grouped[:, None, :]
    position = jnp.arange(block_rows, dtype=jnp.int32)
    earlier = position[None, :] < position[:, None]
    within = jnp.sum((matches & earlier[None]).astype(jnp.int32), axis=2).reshape(-1)
    sources = jnp.arange(blocks * block_rows, dtype=jnp.int32) // block_rows
    return flat_ids * (blocks * MOST) + sources * MOST + within


def shards(
    hidden, base_down_weight, adapter_input_factors, adapter_output_factors, adapter_of_request
):
    adapter_count = lax.axis_size("adapter")
    owner_index = lax.axis_index("adapter")
    rows_local, width_part = hidden.shape
    total_rows = rows_local * adapter_count
    adapters_resident = adapter_input_factors.shape[0]
    every_adapter = adapter_output_factors.shape[0]
    rank_segment = adapter_output_factors.shape[1]
    adapter_wise = adapter_count * MOST
    flat_ids = adapter_of_request[:, 0]
    slot_position = slot_numbers(flat_ids, adapter_count, rows_local)
    slot_row_block = jnp.full((every_adapter * adapter_wise,), -1, jnp.int32)
    slot_row_block = slot_row_block.at[slot_position].set(jnp.arange(total_rows, dtype=jnp.int32))
    gathered = lax.all_gather(hidden, "adapter", axis=0, tiled=True)
    owned = lax.dynamic_slice_in_dim(
        slot_row_block,
        owner_index * adapters_resident * adapter_wise,
        adapters_resident * adapter_wise,
    )
    selected_factor = gathered[jnp.clip(owned, 0, total_rows - 1)]
    selected_factor = jnp.where(
        (owned >= 0)[:, None], selected_factor, jnp.zeros((), selected_factor.dtype)
    )
    selected_factor = selected_factor.reshape(adapters_resident, adapter_wise, width_part)
    rank_partial_sum = jnp.einsum(
        "ndb,nbh->ndh", selected_factor, adapter_input_factors, preferred_element_type=jnp.float32
    )
    rank_mine = lax.psum_scatter(
        rank_partial_sum, "tensor", scatter_dimension=2, tiled=True
    ).astype(jnp.bfloat16)
    rank_all = lax.all_gather(rank_mine.reshape(-1), "adapter", axis=0, tiled=True)
    rank_all = rank_all.reshape(every_adapter * adapter_wise, rank_segment)
    rank_rows = rank_all[slot_position]
    one_hot = (flat_ids[:, None] == jnp.arange(every_adapter, dtype=jnp.int32)[None, :]).astype(
        jnp.bfloat16
    )
    spread = (one_hot[:, :, None] * rank_rows[:, None, :]).reshape(
        total_rows, every_adapter * rank_segment
    )
    output_factor = adapter_output_factors.reshape(
        every_adapter * rank_segment, adapter_output_factors.shape[2]
    )
    base_part = jnp.dot(gathered, base_down_weight, preferred_element_type=jnp.float32)
    summed = lax.psum_scatter(
        base_part + jnp.dot(spread, output_factor, preferred_element_type=jnp.float32),
        "tensor",
        scatter_dimension=0,
        tiled=True,
    )
    return summed.astype(jnp.bfloat16)


def solution(mesh):
    return jax.shard_map(
        shards,
        mesh=mesh,
        in_specs=(
            P(("groups", "adapter"), "tensor"),
            P("tensor", "adapter"),
            P("adapter", "tensor", None),
            P(None, "tensor", "adapter"),
            P("groups", None),
        ),
        out_specs=P(("groups", "tensor"), "adapter"),
        check_vma=False,
    )
```

profile of v0, /device:TPU:0, one launch (start us, length us, event | category | flops | bytes accessed | tf_op | source)
XLA Modules:
  0.0 201.0 jit_solution(14781160947652039038)
XLA Ops:
  6.5 0.0 copy-start
  6.5 0.0 all-gather.2.cloned.1.call-start
  6.5 0.7 all-gather.2.cloned.1.call-update
  7.3 0.0 reduce-scatter.7.cloned.1.call-start
  7.3 1.0 convert_reduce_fusion
  8.3 0.7 compare_select_fusion
  9.0 2.4 %scatter_custom_fusion = s32[512]{0:T(512)S(1)} fusion(s32[512]{0:T(512)S(1)} %bitcast.17, s32[512]{0:T(512)S(1)} %iota.29, s32[]{:T(128)} %constant.13.clone.1), kind=kCustom, calls=%fused_computation.27 | custom fusion | bytes 2052 | tf_op jit(solution)/shard_map/scatter | solution.py:33
  11.5 0.1 broadcast_compare_fusion
  11.6 0.1 broadcast_in_dim.30
  11.7 0.1 compare_select_fusion.1
  11.8 0.7 fusion.8
  12.5 51.5 %all-gather.2.cloned.1.call-done = bf16[512,7168]{1,0:T(8,128)(2,1)} async-done(((bf16[128,7168]{1,0:T(8,128)(2,1)}), bf16[512,7168]{1,0:T(8,128)(2,1)}) %all-gather.2.cloned.1.call-update) | async-done | bytes 7340048 | tf_op jit(solution)/shard_map/all_gather | solution.py:34
  64.0 8.7 %gather_fusion = bf16[128,7168]{1,0:T(8,128)(2,1)} fusion(bf16[512,7168]{1,0:T(8,128)(2,1)} %all-gather.2.cloned.1.call-done, s32[1024]{0:T(1024)S(1)} %pad_clamp_fusion.1), kind=kCustom, calls=%fused_computation | custom fusion | bytes 3670528 | tf_op jit(solution)/shard_map/gather | solution.py:40
  72.7 5.7 %fusion.1 = f32[8,16,64]{2,1,0:T(8,128)S(1)} fusion(bf16[8,7168,64]{1,2,0:T(8,128)(2,1)} %param.7, bf16[8,16,7168]{2,1,0:T(8,128)(2,1)} %bitcast.12, pred[8,16]{1,0:T(8,128)(4,1)S(1)} %broadcast_in_dim.30), kind=kOutput, calls=%fused_computation.5 | convolution fusion | flops 118358016 | bytes 9207936 | tf_op jit(solution)/shard_map/ndb,nbh->ndh/dot_general | solution.py:45
  78.4 0.2 copy.14
  78.6 0.7 reshape.124
  79.3 0.0 reduce-scatter.7.cloned.1.call-update
  79.3 0.0 reduce-scatter.5.cloned.1.call-start
  79.4 22.0 %fusion.15 = f32[512,2048]{1,0:T(8,128)} fusion(bf16[512,7168]{1,0:T(8,128)(2,1)} %all-gather.2.cloned.1.call-done, bf16[7168,2048]{1,0:T(8,128)(2,1)} %param.6), kind=kOutput, calls=%fused_computation.31 | convolution fusion | flops 15032385536 | bytes 40894464 | tf_op jit(solution)/shard_map/dot_general | solution.py:63
  101.4 0.0 reduce-scatter.7.cloned.1.call-done
  101.4 0.8 reshape.125
  102.2 0.1 copy.15
  102.3 0.1 reshape.96
  102.4 5.4 %all_gather.7 = bf16[8192]{0:T(1024)(128)(2,1)S(1)} all-gather(bf16[2048]{0:T(1024)(128)(2,1)S(1)} %reshape.96), channel_id=1, replica_groups=mesh['groups'=2,'adapter'=4,'tensor'=4] {'adapter'}, dimensions={0}, use_global_device_ids=true | all-gather | bytes 20480 | tf_op jit(solution)/shard_map/all_gather | solution.py:51
  107.8 0.1 reshape.97
  107.9 1.3 gather_fusion.1
  109.2 0.1 copy.12
  109.3 0.0 copy-done
  109.3 6.1 %bitcast_add_fusion = f32[512,2048]{1,0:T(8,128)} fusion(f32[512,2048]{1,0:T(8,128)} %fusion.15, bf16[32,16,2048]{2,1,0:T(8,128)(2,1)S(1)} %copy-done, bf16[512,16]{0,1:T(8,128)(2,1)S(1)} %copy.12, bf16[512,32]{0,1:T(8,128)(2,1)S(1)} %fusion.8), kind=kOutput, calls=%fused_computation.3 | convolution fusion | flops 1075052544 | bytes 10534912 | tf_op jit(solution)/shard_map/dot_general | solution.py:65
  115.4 0.0 reduce-scatter.5.cloned.1.call-update
  115.5 76.9 %reduce-scatter.5.cloned.1.call-done = f32[128,2048]{1,0:T(8,128)} async-done(((f32[512,2048]{1,0:T(8,128)}), f32[128,2048]{1,0:T(8,128)}) %reduce-scatter.5.cloned.1.call-update) | async-done | bytes 1048592 | tf_op jit(solution)/shard_map/reduce_scatter | solution.py:64
  192.4 2.1 %convert_element_type.19 = bf16[128,2048]{1,0:T(8,128)(2,1)} convert(f32[128,2048]{1,0:T(8,128)} %reduce-scatter.5.cloned.1.call-done) | non-fusion elementwise | flops 262144 | bytes 1572864 | tf_op jit(solution)/shard_map/convert_element_type | solution.py:70
  (4 shorter events, 0.0 us)
Async XLA Ops:
  6.5 102.8 %copy-start = (bf16[32,16,2048]{2,1,0:T(8,128)(2,1)S(1)}, bf16[32,16,2048]{2,1,0:T(8,128)(2,1)}, u32[]{:S(2)}) copy-start(bf16[32,16,2048]{2,1,0:T(8,128)(2,1)} %param.8) | copy-start | bytes 6291460
  6.5 57.4 %all-gather.2.cloned.1.call-start = ((), (), s32[]{:S(2)}) async-start(), calls=%async_computation.2 | async-start | bytes 9175040 | tf_op jit(solution)/shard_map/all_gather | solution.py:34
  7.3 94.2 %reduce-scatter.7.cloned.1.call-start = ((), (), s32[]{:S(2)}) async-start(), calls=%async_computation.4 | async-start | bytes 40960
  79.3 113.0 %reduce-scatter.5.cloned.1.call-start = ((), (), s32[]{:S(2)}) async-start(), calls=%async_computation.3 | async-start | bytes 5242880 | tf_op jit(solution)/shard_map/reduce_scatter | solution.py:64
Sparse Core Ops, SparseCore 0:
  8.9 55.0 all-gather.1
  79.5 18.9 reduce-scatter.6
  115.6 76.7 reduce-scatter.4
where the time goes:
time: 201 us
  waiting for transfers between devices  129 us (64%)
  matrix products  33.8 us (17%)
  local copies, waits for them, and re-layouts  14.7 us (7%)
  between operations  13.2 us (7%)
  blocking collectives  5.36 us (3%)
  other arithmetic  4.66 us (2%)
    reduce_scatter x1, waiting for transfers between devices, shards(): lax.psum_scatter(base_part + jnp.dot(spread, output_factor, preferred_ele...  76.9 us
    all_gather x1, waiting for transfers between devices, shards(): gathered = lax.all_gather(hidden, 'adapter', axis=0, tiled=True)  51.5 us
    dot_general x1, matrix products, shards(): jnp.dot(gathered, base_down_weight, preferred_element_type=jnp.float32)  22 us
    gather x1, local copies, waits for them, and re-layouts, shards(): selected_factor = gathered[jnp.clip(owned, 0, total_rows - 1)]  8.72 us
    dot_general x1, matrix products, shards(): jnp.dot(spread, output_factor, preferred_element_type=jnp.float32)  6.1 us
    dot_general x1, matrix products, shards(): jnp.einsum('ndb,nbh->ndh', selected_factor, adapter_input_factors, prefer...  5.7 us
    all_gather x1, blocking collectives, shards(): lax.all_gather(rank_mine.reshape(-1), 'adapter', axis=0, tiled=True)  5.36 us
  transfers between devices with their start and end apart: 3, of which 2 were waited for; matrix products, arithmetic and copies ran while one was open for 13% of the time, Pallas kernels for 0%

commit v1 on v0

v1 whole, which is shorter than its diff:
```python
import jax
import jax.numpy as jnp
from jax import lax
from jax.sharding import PartitionSpec as P


def shards(
    hidden, base_down_weight, adapter_input_factors, adapter_output_factors, adapter_of_request
):
    owner_index = lax.axis_index("adapter")
    adapters_resident = adapter_input_factors.shape[0]
    every_adapter = adapter_output_factors.shape[0]
    rank_segment = adapter_output_factors.shape[1]
    flat_ids = adapter_of_request[:, 0]
    total_rows = flat_ids.shape[0]
    gathered = lax.all_gather(hidden, "adapter", axis=0, tiled=True)
    dense = jnp.einsum(
        "rb,nbh->rnh", gathered, adapter_input_factors, preferred_element_type=jnp.float32
    )
    here = owner_index * adapters_resident + jnp.arange(adapters_resident, dtype=jnp.int32)
    owned = flat_ids[:, None] == here[None, :]
    low_part = jnp.sum(jnp.where(owned[:, :, None], dense, 0.0), axis=1)
    low_mine = lax.psum_scatter(
        low_part, "tensor", scatter_dimension=1, tiled=True
    ).astype(jnp.bfloat16)
    low_rows = lax.psum(low_mine, "adapter")
    one_hot = flat_ids[:, None] == jnp.arange(every_adapter, dtype=jnp.int32)[None, :]
    spread = jnp.where(one_hot[:, :, None], low_rows[:, None, :], jnp.zeros((), jnp.bfloat16))
    spread = spread.reshape(total_rows, every_adapter * rank_segment)
    output_factor = adapter_output_factors.reshape(
        every_adapter * rank_segment, adapter_output_factors.shape[2]
    )
    base_part = jnp.dot(gathered, base_down_weight, preferred_element_type=jnp.float32)
    part = base_part + jnp.dot(spread, output_factor, preferred_element_type=jnp.float32)
    return lax.psum_scatter(
        part.astype(jnp.bfloat16), "tensor", scatter_dimension=0, tiled=True
    )


def solution(mesh):
    return jax.shard_map(
        shards,
        mesh=mesh,
        in_specs=(
            P(("groups", "adapter"), "tensor"),
            P("tensor", "adapter"),
            P("adapter", "tensor", None),
            P(None, "tensor", "adapter"),
            P("groups", None),
        ),
        out_specs=P(("groups", "tensor"), "adapter"),
        check_vma=False,
    )
```

time: 201 us -> 164 us (0.82)
  waiting for transfers between devices: 129 us -> 101 us
  local copies, waits for them, and re-layouts: 14.7 us -> 0.01 us
  blocking collectives: 5.36 us -> 10.3 us
    reduce_scatter x1 -> x2, waiting for transfers between devices: 76.9 us -> 45.1 us  [the longest x1 45.1 us: shards(): lax.psum_scatter(part.astype(jnp.bfloat16), 'tensor', scatter_dimension=0...]
    psum x0 -> x1, blocking collectives: none -> 10.3 us  [shards(): low_rows = lax.psum(low_mine, 'adapter')]
    gather x3 -> x0, local copies, waits for them, and re-layouts: 10.1 us -> none  [the longest x1 8.72 us: shards(): selected_factor = gathered[jnp.clip(owned, 0, total_rows - 1)]]
    unnamed x0 -> x1, matrix products: none -> 8.42 us
    dot_general x1 -> x0, matrix products: 5.7 us -> none  [shards(): jnp.einsum('ndb,nbh->ndh', selected_factor, adapter_input_factors, prefer...]
    all_gather x1 -> x0, blocking collectives: 5.36 us -> none  [shards(): lax.all_gather(rank_mine.reshape(-1), 'adapter', axis=0, tiled=True)]
    all_gather x1, waiting for transfers between devices: 51.5 us -> 55.2 us  [shards(): gathered = lax.all_gather(hidden, 'adapter', axis=0, tiled=True)]
    scatter x1 -> x0, local copies, waits for them, and re-layouts: 2.44 us -> none  [shards(): slot_row_block.at[slot_position]]
  transfers between devices with their start and end apart: 3 -> 3, of which waited for: 2 -> 2; matrix products, arithmetic and copies ran while one was open for 13% -> 14% of each run, Pallas kernels for 0% -> 0%
where the time goes in v1:
time: 164 us; the launch traced here: 163 us
  waiting for transfers between devices  101 us (62%)
  matrix products  35.8 us (22%)
  between operations  13.1 us (8%)
  blocking collectives  10.3 us (6%)
  other arithmetic  2.99 us (2%)
    all_gather x1, waiting for transfers between devices, shards(): gathered = lax.all_gather(hidden, 'adapter', axis=0, tiled=True)  55.2 us
    reduce_scatter x1, waiting for transfers between devices, shards(): lax.psum_scatter(part.astype(jnp.bfloat16), 'tensor', scatter_dimension=0...  45.1 us
    dot_general x1, matrix products, shards(): jnp.dot(gathered, base_down_weight, preferred_element_type=jnp.float32)  22 us
    psum x1, blocking collectives, shards(): low_rows = lax.psum(low_mine, 'adapter')  10.3 us
    unnamed x1, matrix products  8.42 us
    dot_general x1, matrix products, shards(): jnp.dot(spread, output_factor, preferred_element_type=jnp.float32)  5.33 us
  transfers between devices with their start and end apart: 3, of which 2 were waited for; matrix products, arithmetic and copies ran while one was open for 14% of the time, Pallas kernels for 0%

profile of v1, /device:TPU:0, one launch (start us, length us, event | category | flops | bytes accessed | tf_op | source)
XLA Modules:
  0.0 163.3 jit_solution(15520611946354408500)
XLA Ops:
  6.5 0.0 copy-start
  6.5 0.0 all-gather.2.cloned.1.call-start
  6.5 0.7 all-gather.2.cloned.1.call-update
  7.3 0.0 reduce-scatter.3.cloned.1.call-start
  7.3 0.8 broadcast_compare_fusion
  8.1 0.7 iota_compare_fusion
  8.8 55.2 %all-gather.2.cloned.1.call-done = bf16[512,7168]{1,0:T(8,128)(2,1)} async-done(((bf16[128,7168]{1,0:T(8,128)(2,1)}), bf16[512,7168]{1,0:T(8,128)(2,1)}) %all-gather.2.cloned.1.call-update) | async-done | bytes 7340048 | tf_op jit(solution)/shard_map/all_gather | solution.py:16
  64.0 8.4 %fusion.8 = f32[512,512]{0,1:S(1)} fusion(bf16[512,7168]{1,0:T(8,128)(2,1)} %all-gather.2.cloned.1.call-done, bf16[7168,512]{0,1:T(8,128)(2,1)} %bitcast.16), kind=kOutput, calls=%fused_computation.13 | convolution fusion | flops 3758096384 | bytes 15728640
  72.4 0.8 select_reduce_fusion
  73.2 0.0 reduce-scatter.3.cloned.1.call-update
  73.2 0.0 reduce-scatter.5.cloned.1.call-start
  73.3 22.0 %fusion.7 = f32[512,2048]{1,0:T(8,128)} fusion(bf16[512,7168]{1,0:T(8,128)(2,1)} %all-gather.2.cloned.1.call-done, bf16[7168,2048]{1,0:T(8,128)(2,1)} %param.6), kind=kOutput, calls=%fused_computation.12 | convolution fusion | flops 15032385536 | bytes 40894464 | tf_op jit(solution)/shard_map/dot_general | solution.py:33
  95.3 0.0 reduce-scatter.3.cloned.1.call-done
  95.3 0.8 convert_element_type.6
  96.1 10.3 %psum.7 = bf16[512,16]{0,1:T(8,128)(2,1)S(1)} all-reduce(bf16[512,16]{0,1:T(8,128)(2,1)S(1)} %convert_element_type.6), channel_id=1, replica_groups=mesh['groups'=2,'adapter'=4,'tensor'=4] {'adapter'}, use_global_device_ids=true, to_apply=%region_2.3 | all-reduce | flops 8192 | bytes 32768 | tf_op jit(solution)/shard_map/psum | solution.py:26
  106.3 0.0 copy-done
  106.3 5.3 %fusion = bf16[512,2048]{1,0:T(8,128)(2,1)} fusion(f32[512,2048]{1,0:T(8,128)} %fusion.7, bf16[32,16,2048]{2,1,0:T(8,128)(2,1)S(1)} %copy-done, pred[512,32]{0,1:T(8,128)(4,1)S(1)} %iota_compare_fusion, bf16[512,16]{0,1:T(8,128)(2,1)S(1)} %psum.7), kind=kOutput, calls=%fused_computation.1 | convolution fusion | flops 1076101120 | bytes 8421376 | tf_op jit(solution)/shard_map/dot_general | solution.py:34
  111.6 0.0 reduce-scatter.5.cloned.1.call-update
  111.7 45.1 %reduce-scatter.5.cloned.1.call-done = bf16[128,2048]{1,0:T(8,128)(2,1)} async-done(((bf16[512,2048]{1,0:T(8,128)(2,1)}), bf16[128,2048]{1,0:T(8,128)(2,1)}) %reduce-scatter.5.cloned.1.call-update) | async-done | bytes 524304 | tf_op jit(solution)/shard_map/reduce_scatter | solution.py:35
  (1 shorter events, 0.0 us)
Async XLA Ops:
  6.5 99.8 %copy-start = (bf16[32,16,2048]{2,1,0:T(8,128)(2,1)S(1)}, bf16[32,16,2048]{2,1,0:T(8,128)(2,1)}, u32[]{:S(2)}) copy-start(bf16[32,16,2048]{2,1,0:T(8,128)(2,1)} %param.8) | copy-start | bytes 6291460
  6.5 57.4 %all-gather.2.cloned.1.call-start = ((), (), s32[]{:S(2)}) async-start(), calls=%async_computation.2 | async-start | bytes 9175040 | tf_op jit(solution)/shard_map/all_gather | solution.py:16
  7.3 88.0 %reduce-scatter.3.cloned.1.call-start = ((), (), s32[]{:S(2)}) async-start(), calls=%async_computation.3 | async-start | bytes 163840 | tf_op jit(solution)/shard_map/reduce_scatter | solution.py:23
  73.2 83.5 %reduce-scatter.5.cloned.1.call-start = ((), (), s32[]{:S(2)}) async-start(), calls=%async_computation.4 | async-start | bytes 2621440 | tf_op jit(solution)/shard_map/reduce_scatter | solution.py:35
Sparse Core Ops, SparseCore 0:
  8.9 55.0 all-gather.1
  73.3 19.1 reduce-scatter.2
  111.8 44.9 reduce-scatter.4

commit v2 on v1

v2 whole, which is shorter than its diff:
```python
import functools
import jax
import jax.numpy as jnp
from jax import lax
from jax.experimental import pallas as pl
from jax.experimental.pallas import tpu as pltpu
from jax.sharding import PartitionSpec as P

CHUNK = 32
TILE = 256
F32 = jnp.float32
BF16 = jnp.bfloat16


def kernel(
    na, nt, ids_ref, hidden, weight, in_t, out_f, out_ref,
    w_v, in_v, of_v, rows_v, acc, low_mine, low_recv, bc_mine, bc_recv, rs_mine, rs_recv,
    load_sem, x_ss, x_rs, core_ss, core_rs, fwd_ss, fwd_rs,
    low_ss, low_rs, bc_ss, bc_rs, rs_ss, rs_rs,
):
    rounds, _, chunk, depth = rows_v.shape
    chips = na // 2
    per = na // nt
    width = weight.shape[1]
    total = na * chunk
    residents = in_t.shape[0] // (nt * low_mine.shape[2])
    rank = nt * low_mine.shape[2]
    seg = low_mine.shape[2]
    every = out_f.shape[0] // seg
    me_a = lax.axis_index("adapter")
    me_t = lax.axis_index("tensor")
    core = lax.rem(me_a, 2)
    chip = me_a // 2
    partner = me_a + 1 - 2 * core

    def to_a(a):
        return {"adapter": a}

    def to_t(t):
        return {"tensor": t}

    def rdma(src, dst, ss, rs, dev):
        return pltpu.make_async_remote_copy(
            src_ref=src, dst_ref=dst, send_sem=ss, recv_sem=rs,
            device_id=dev, device_id_type=pl.DeviceIdType.MESH,
        )

    loads = [
        pltpu.make_async_copy(hidden, rows_v.at[:, me_a], load_sem.at[0]),
        pltpu.make_async_copy(in_t, in_v, load_sem.at[1]),
        pltpu.make_async_copy(weight, w_v, load_sem.at[2]),
        pltpu.make_async_copy(out_f, of_v, load_sem.at[3]),
    ]

    barrier = pltpu.get_barrier_semaphore()
    for d in range(1, na):
        pl.semaphore_signal(
            barrier, inc=1, device_id=to_a(lax.rem(me_a + d, na)),
            device_id_type=pl.DeviceIdType.MESH,
        )
    for d in range(1, nt):
        pl.semaphore_signal(
            barrier, inc=1, device_id=to_t(lax.rem(me_t + d, nt)),
            device_id_type=pl.DeviceIdType.MESH,
        )
    loads[0].start()
    loads[1].start()
    pl.semaphore_wait(barrier, na - 1 + nt - 1)

    def x_send(i, d):
        there = lax.rem(chip + d, chips) * 2 + core
        return rdma(
            hidden.at[i], rows_v.at[i, me_a], x_ss.at[i, d], x_rs.at[i, d], to_a(there)
        )

    def core_send(i):
        return rdma(
            hidden.at[i], rows_v.at[i, me_a], core_ss.at[i], core_rs.at[i], to_a(partner)
        )

    def fwd_send(i, d):
        block = lax.rem(chip + chips - d, chips) * 2 + core
        return rdma(
            rows_v.at[i, block], rows_v.at[i, block],
            fwd_ss.at[i, d], fwd_rs.at[i, d], to_a(partner),
        )

    def low_send(i, d):
        t = lax.rem(me_t + d, nt)
        return rdma(
            low_mine.at[i, t], low_recv.at[i, d], low_ss.at[i, d], low_rs.at[i, d], to_t(t)
        )

    def bc_send(i, d):
        a = lax.rem(me_a + d, na)
        return rdma(
            bc_mine.at[i], bc_recv.at[i, d], bc_ss.at[i, d], bc_rs.at[i, d], to_a(a)
        )

    def rs_send(i, d):
        t = lax.rem(me_t + d, nt)
        return rdma(
            rs_mine.at[i, t], rs_recv.at[i, d], rs_ss.at[i, d], rs_rs.at[i, d], to_t(t)
        )

    for i in range(min(2, rounds)):
        for d in range(1, chips):
            x_send(i, d).start()
        core_send(i).start()
    loads[2].start()
    loads[3].start()
    for i in range(2, rounds):
        core_send(i).start()

    def front(i):
        for d in range(1, chips):
            x_send(i, d).wait_recv()
            fwd_send(i, d).start()
        for d in range(1, chips):
            x_send(i, d).wait_send()

        @pl.when(i + 2 < rounds)
        def _():
            for d in range(1, chips):
                x_send(i + 2, d).start()

    def middle(i, first):
        core_send(i).wait_recv()
        for d in range(1, chips):
            fwd_send(i, d).wait_recv()
        if first:
            loads[0].wait()
            loads[1].wait()
        ids = ids_ref[i]
        low = jnp.zeros((rank, total), F32)
        here = rows_v[i].reshape(total, depth)
        projected = lax.dot_general(
            in_v[...], here, (((1,), (1,)), ((), ())), preferred_element_type=F32
        )
        for n in range(residents):
            low = low + jnp.where(
                ids == me_a * residents + n, projected[n * rank:(n + 1) * rank], 0.0
            )
        low_mine[i] = low.reshape(nt, seg, total)
        for d in range(1, nt):
            low_send(i, d).start()
        if first:
            loads[2].wait()
            loads[3].wait()

        def tile(j, carry):
            cols = pl.ds(pl.multiple_of(j * TILE, TILE), TILE)
            part = jnp.dot(
                rows_v[i].reshape(total, depth), w_v[:, cols], preferred_element_type=F32
            )
            acc[i, :, :, cols] = part.reshape(nt, per * chunk, TILE)
            return carry

        lax.fori_loop(0, width // TILE, tile, 0)
        summed = low_mine[i, me_t]
        for d in range(1, nt):
            low_send(i, d).wait_recv()
            summed = summed + low_recv[i, d]
        bc_mine[i] = summed.astype(BF16).astype(F32)
        for d in range(1, na):
            bc_send(i, d).start()

    def back(i):
        rows_low = bc_mine[i]
        for d in range(1, na):
            bc_send(i, d).wait_recv()
            rows_low = rows_low + bc_recv[i, d]
        ids = ids_ref[i]
        which = lax.broadcasted_iota(jnp.int32, (every, 1, total), 0)
        spread = jnp.where(which == ids[None], rows_low[None], 0.0)
        spread = spread.reshape(every * seg, total).T.astype(BF16)

        def tile(j, carry):
            cols = pl.ds(pl.multiple_of(j * TILE, TILE), TILE)
            part = jnp.dot(spread, of_v[:, cols], preferred_element_type=F32)
            part = acc[i, :, :, cols] + part.reshape(nt, per * chunk, TILE)
            acc[i, :, :, cols] = part
            rs_mine[i, :, :, cols] = part.astype(BF16)
            return carry

        lax.fori_loop(0, width // TILE, tile, 0)
        for d in range(1, nt):
            rs_send(i, d).start()

    front(0)
    middle(0, True)

    def body(i, carry):
        front(i)
        back(i - 1)
        middle(i, False)
        return carry

    lax.fori_loop(1, rounds, body, 0)
    back(rounds - 1)

    def finish(i, carry):
        val = acc[i, me_t]
        for d in range(1, nt):
            rs_send(i, d).wait_recv()
            val = val + rs_recv[i, d].astype(F32)
        out_ref[:, i] = val.reshape(per, chunk, width).astype(BF16)
        for d in range(1, chips):
            fwd_send(i, d).wait_send()
        core_send(i).wait_send()
        for d in range(1, nt):
            low_send(i, d).wait_send()
            rs_send(i, d).wait_send()
        for d in range(1, na):
            bc_send(i, d).wait_send()
        return carry

    lax.fori_loop(0, rounds, finish, 0)


def shards(na, nt, hidden, weight, in_f, out_f, ids):
    rows_local, depth = hidden.shape
    width = weight.shape[1]
    residents, _, rank = in_f.shape
    every, seg, _ = out_f.shape
    chunk = CHUNK
    rounds = rows_local // chunk
    per = na // nt
    chips = na // 2
    total = na * chunk
    in_t = jnp.transpose(in_f, (0, 2, 1)).reshape(residents * rank, depth)
    out_f = out_f.reshape(every * seg, width)
    ids = ids.reshape(na, rounds, chunk).transpose(1, 0, 2).reshape(rounds, 1, total)
    hidden = hidden.reshape(rounds, chunk, depth)
    dma = pltpu.SemaphoreType.DMA
    anywhere = pl.BlockSpec(memory_space=pl.ANY)
    vmem = pl.BlockSpec(memory_space=pltpu.VMEM)
    flops = 2 * na * rows_local * depth * (width + residents * rank)
    out = pl.pallas_call(
        functools.partial(kernel, na, nt),
        out_shape=jax.ShapeDtypeStruct((per, rounds, chunk, width), BF16),
        in_specs=[vmem, anywhere, anywhere, anywhere, anywhere],
        out_specs=vmem,
        scratch_shapes=[
            pltpu.VMEM((depth, width), BF16),
            pltpu.VMEM((residents * rank, depth), BF16),
            pltpu.VMEM((every * seg, width), BF16),
            pltpu.VMEM((rounds, na, chunk, depth), BF16),
            pltpu.VMEM((rounds, nt, per * chunk, width), F32),
            pltpu.VMEM((rounds, nt, seg, total), F32),
            pltpu.VMEM((rounds, nt, seg, total), F32),
            pltpu.VMEM((rounds, seg, total), F32),
            pltpu.VMEM((rounds, na, seg, total), F32),
            pltpu.VMEM((rounds, nt, per * chunk, width), BF16),
            pltpu.VMEM((rounds, nt, per * chunk, width), BF16),
            dma((4,)),
            dma((rounds, chips)), dma((rounds, chips)),
            dma((rounds,)), dma((rounds,)),
            dma((rounds, chips)), dma((rounds, chips)),
            dma((rounds, nt)), dma((rounds, nt)),
            dma((rounds, na)), dma((rounds, na)),
            dma((rounds, nt)), dma((rounds, nt)),
        ],
        compiler_params=pltpu.CompilerParams(
            collective_id=0, has_side_effects=True, vmem_limit_bytes=63 * 1024 * 1024
        ),
        cost_estimate=pl.CostEstimate(
            flops=flops, bytes_accessed=2 * depth * width, transcendentals=0
        ),
    )(ids, hidden, weight, in_t, out_f)
    return out.reshape(per * rows_local, width)


def solution(mesh):
    return jax.shard_map(
        functools.partial(shards, mesh.shape["adapter"], mesh.shape["tensor"]),
        mesh=mesh,
        in_specs=(
            P(("groups", "adapter"), "tensor"),
            P("tensor", "adapter"),
            P("adapter", "tensor", None),
            P(None, "tensor", "adapter"),
            P("groups", None),
        ),
        out_specs=P(("groups", "tensor"), "adapter"),
        check_vma=False,
    )
```

time: 164 us -> 112 us (0.68)
  Pallas kernels: 0 us -> 108 us
  waiting for transfers between devices: 101 us -> 0 us
  matrix products: 35.8 us -> 0 us
  between operations: 13.1 us -> 0.01 us
  blocking collectives: 10.3 us -> 0 us
  local copies, waits for them, and re-layouts: 0.01 us -> 3.15 us
  other arithmetic: 2.99 us -> 1.34 us
    pallas_call x0 -> x1, Pallas kernels: none -> 108 us  [shards(): pl.pallas_call(functools.partial(kernel, na, nt), out_shape=jax.ShapeDtyp...]
    all_gather x1 -> x0, waiting for transfers between devices: 55.2 us -> none  [shards(): gathered = lax.all_gather(hidden, 'adapter', axis=0, tiled=True)]
    reduce_scatter x2 -> x0, waiting for transfers between devices: 45.1 us -> none  [the longest x1 45.1 us: shards(): lax.psum_scatter(part.astype(jnp.bfloat16), 'tensor', scatter_dimension=0...]
    dot_general x2 -> x0, matrix products: 27.4 us -> none  [the longest x1 22 us: shards(): jnp.dot(gathered, base_down_weight, preferred_element_type=jnp.float32)]
    psum x1 -> x0, blocking collectives: 10.3 us -> none  [shards(): low_rows = lax.psum(low_mine, 'adapter')]
    unnamed x1 -> x0, matrix products: 8.42 us -> none
    unnamed x2, local copies, waits for them, and re-layouts: 0.01 us -> 2.39 us
  transfers between devices with their start and end apart: 3 -> 0, of which waited for: 2 -> 0; matrix products, arithmetic and copies ran while one was open for 14% -> 0% of each run, Pallas kernels for 0% -> 0%
where the time goes in v2:
time: 112 us
  Pallas kernels  108 us (96%)
  local copies, waits for them, and re-layouts  3.15 us (3%)
  other arithmetic  1.34 us (1%)
    pallas_call x1, Pallas kernels, shards(): pl.pallas_call(functools.partial(kernel, na, nt), out_shape=jax.ShapeDtyp...  108 us
    unnamed x2, local copies, waits for them, and re-layouts  2.39 us

profile of v2, /device:TPU:0, one launch (start us, length us, event | category | flops | bytes accessed | tf_op | source)
XLA Modules:
  0.0 112.0 jit_solution(7088494634899361451)
XLA Ops:
  0.0 0.5 broadcast.3
  0.5 1.3 %reduce.3 = s32[512]{0:T(512)S(1)} reduce(s32[512,1]{0,1:T(1,128)} %param.9, s32[]{:T(128)} %broadcast.3), dimensions={1}, to_apply=%param.9.reduce_sub_computation.3 | reduce | bytes 4100 | tf_op args[4]
  1.9 0.1 reshape.18
  1.9 0.7 reshape.19.ids_ref
  2.6 107.5 %shard_map.55 = bf16[1,4,32,2048]{3,2,1,0:T(8,128)(2,1)} custom-call(s32[4,1,128]{2,1,0:T(1,128)} %reshape.19.ids_ref, bf16[4,32,7168]{2,1,0:T(8,128)(2,1)} %bitcast.14, bf16[7168,2048]{1,0:T(8,128)(2,1)} %weight.1, bf16[512,7168]{1,0:T(8,128)(2,1)} %bitcast.12, bf16[512,2048]{1,0:T(8,128)(2,1)} %bitcast.13), custom_call_target="tpu_custom_call" | custom-call | flops 18790481920 | bytes 29360128 | tf_op jit(solution)/shard_map/pallas_call | solution.py:239
  110.1 1.9 %copy.10 = bf16[128,2048]{1,0:T(8,128)(2,1)} copy(bf16[128,2048]{1,0:T(8,128)(2,1)} %bitcast.10) | data formatting | bytes 1048576
  (1 shorter events, 0.0 us)

commit v3 on v2

--- a/solution.py
+++ b/solution.py
@@ -16,7 +16,7 @@
     na, nt, ids_ref, hidden, weight, in_t, out_f, out_ref,
     w_v, in_v, of_v, rows_v, acc, low_mine, low_recv, bc_mine, bc_recv, rs_mine, rs_recv,
     load_sem, x_ss, x_rs, core_ss, core_rs, fwd_ss, fwd_rs,
-    low_ss, low_rs, bc_ss, bc_rs, rs_ss, rs_rs,
+    low_ss, low_rs, bc_ss, bc_rs, rs_ss, rs_rs, *hop,
 ):
     rounds, _, chunk, depth = rows_v.shape
     chips = na // 2
@@ -32,6 +32,13 @@
     core = lax.rem(me_a, 2)
     chip = me_a // 2
     partner = me_a + 1 - 2 * core
+    two_hop = nt == 4
+    if two_hop:
+        hop_recv, hop_ss, hop_rs = hop
+        near = me_t + 1 - 2 * lax.rem(me_t, 2)
+        far = 2 - 2 * (me_t // 2)
+        outer = lax.rem(me_t, nt - 1) == 0
+        inner = lax.rem(me_t, nt - 1) != 0
 
     def to_a(a):
         return {"adapter": a}
@@ -103,14 +110,28 @@
             rs_mine.at[i, t], rs_recv.at[i, d], rs_ss.at[i, d], rs_rs.at[i, d], to_t(t)
         )
 
-    for i in range(min(2, rounds)):
-        for d in range(1, chips):
-            x_send(i, d).start()
-        core_send(i).start()
+    def near_send(i):
+        return rdma(
+            rs_mine.at[i, near], rs_recv.at[i, 1], rs_ss.at[i, 1], rs_rs.at[i, 1], to_t(near)
+        )
+
+    def hop_send(i, k):
+        return rdma(
+            rs_mine.at[i, far + k], hop_recv.at[i, k], hop_ss.at[i, k], hop_rs.at[i, k],
+            to_t(near),
+        )
+
+    def far_send(i, k):
+        return rdma(
+            rs_mine.at[i, far + k], rs_recv.at[i, 2], rs_ss.at[i, 2 + k], rs_rs.at[i, 2],
+            to_t(far + k),
+        )
+
+    for d in range(1, chips):
+        x_send(0, d).start()
+    core_send(0).start()
     loads[2].start()
     loads[3].start()
-    for i in range(2, rounds):
-        core_send(i).start()
 
     def front(i):
         for d in range(1, chips):
@@ -119,10 +140,11 @@
         for d in range(1, chips):
             x_send(i, d).wait_send()
 
-        @pl.when(i + 2 < rounds)
+        @pl.when(i + 1 < rounds)
         def _():
             for d in range(1, chips):
-                x_send(i + 2, d).start()
+                x_send(i + 1, d).start()
+            core_send(i + 1).start()
 
     def middle(i, first):
         core_send(i).wait_recv()
@@ -184,33 +206,74 @@
             return carry
 
         lax.fori_loop(0, width // TILE, tile, 0)
-        for d in range(1, nt):
-            rs_send(i, d).start()
+        if not two_hop:
+            for d in range(1, nt):
+                rs_send(i, d).start()
+            return
+
+        @pl.when(outer)
+        def _():
+            for k in range(2):
+                hop_send(i, k).start()
+
+        near_send(i).start()
+
+    def relay(i):
+        if not two_hop:
+            return
+
+        @pl.when(inner)
+        def _():
+            for k in range(1, -1, -1):
+                hop_send(i, k).wait_recv()
+                joined = acc[i, far + k] + hop_recv[i, k].astype(F32)
+                rs_mine[i, far + k] = joined.astype(BF16)
+                far_send(i, k).start()
 
     front(0)
     middle(0, True)
+    back(0)
 
     def body(i, carry):
         front(i)
-        back(i - 1)
         middle(i, False)
+        relay(i - 1)
+        back(i)
         return carry
 
     lax.fori_loop(1, rounds, body, 0)
-    back(rounds - 1)
+    relay(rounds - 1)
 
     def finish(i, carry):
         val = acc[i, me_t]
-        for d in range(1, nt):
-            rs_send(i, d).wait_recv()
-            val = val + rs_recv[i, d].astype(F32)
+        if two_hop:
+            near_send(i).wait_recv()
+            far_send(i, 0).wait_recv()
+            val = val + (rs_recv[i, 1].astype(F32) + rs_recv[i, 2].astype(F32))
+        else:
+            for d in range(1, nt):
+                rs_send(i, d).wait_recv()
+                val = val + rs_recv[i, d].astype(F32)
         out_ref[:, i] = val.reshape(per, chunk, width).astype(BF16)
         for d in range(1, chips):
             fwd_send(i, d).wait_send()
         core_send(i).wait_send()
         for d in range(1, nt):
             low_send(i, d).wait_send()
-            rs_send(i, d).wait_send()
+            if not two_hop:
+                rs_send(i, d).wait_send()
+        if two_hop:
+            near_send(i).wait_send()
+
+            @pl.when(outer)
+            def _():
+                for k in range(2):
+                    hop_send(i, k).wait_send()
+
+            @pl.when(inner)
+            def _():
+                for k in range(2):
+                    far_send(i, k).wait_send()
         for d in range(1, na):
             bc_send(i, d).wait_send()
         return carry
@@ -233,6 +296,12 @@
     ids = ids.reshape(na, rounds, chunk).transpose(1, 0, 2).reshape(rounds, 1, total)
     hidden = hidden.reshape(rounds, chunk, depth)
     dma = pltpu.SemaphoreType.DMA
+    hop = []
+    if nt == 4:
+        hop = [
+            pltpu.VMEM((rounds, 2, per * chunk, width), BF16),
+            dma((rounds, 2)), dma((rounds, 2)),
+        ]
     anywhere = pl.BlockSpec(memory_space=pl.ANY)
     vmem = pl.BlockSpec(memory_space=pltpu.VMEM)
     flops = 2 * na * rows_local * depth * (width + residents * rank)
@@ -260,7 +329,7 @@
             dma((rounds, nt)), dma((rounds, nt)),
             dma((rounds, na)), dma((rounds, na)),
             dma((rounds, nt)), dma((rounds, nt)),
-        ],
+        ] + hop,
         compiler_params=pltpu.CompilerParams(
             collective_id=0, has_side_effects=True, vmem_limit_bytes=63 * 1024 * 1024
         ),

time: 112 us -> 103 us (0.920)
  Pallas kernels: 108 us -> 97.8 us
    pallas_call x1, Pallas kernels: 108 us -> 97.8 us  [shards(): pl.pallas_call(functools.partial(kernel, na, nt), out_shape=jax.ShapeDtyp...]
where the time goes in v3:
time: 103 us; the launch traced here: 102 us
  Pallas kernels  97.8 us (95%)
  local copies, waits for them, and re-layouts  3.15 us (3%)
  other arithmetic  1.34 us (1%)
    pallas_call x1, Pallas kernels, shards(): pl.pallas_call(functools.partial(kernel, na, nt), out_shape=jax.ShapeDtyp...  97.8 us
    unnamed x2, local copies, waits for them, and re-layouts  2.39 us

profile of v3, /device:TPU:0, one launch (start us, length us, event | category | flops | bytes accessed | tf_op | source)
XLA Modules:
  0.0 102.3 jit_solution(1672255330357365380)
XLA Ops:
  0.0 0.5 broadcast.3
  0.5 1.3 %reduce.3 = s32[512]{0:T(512)S(1)} reduce(s32[512,1]{0,1:T(1,128)} %param.9, s32[]{:T(128)} %broadcast.3), dimensions={1}, to_apply=%param.9.reduce_sub_computation.3 | reduce | bytes 4100 | tf_op args[4]
  1.9 0.1 reshape.18
  1.9 0.7 reshape.19.ids_ref
  2.6 97.8 %shard_map.55 = bf16[1,4,32,2048]{3,2,1,0:T(8,128)(2,1)} custom-call(s32[4,1,128]{2,1,0:T(1,128)} %reshape.19.ids_ref, bf16[4,32,7168]{2,1,0:T(8,128)(2,1)} %bitcast.14, bf16[7168,2048]{1,0:T(8,128)(2,1)} %weight.1, bf16[512,7168]{1,0:T(8,128)(2,1)} %bitcast.12, bf16[512,2048]{1,0:T(8,128)(2,1)} %bitcast.13), custom_call_target="tpu_custom_call" | custom-call | flops 18790481920 | bytes 29360128 | tf_op jit(solution)/shard_map/pallas_call | solution.py:308
  100.4 1.9 %copy.10 = bf16[128,2048]{1,0:T(8,128)(2,1)} copy(bf16[128,2048]{1,0:T(8,128)(2,1)} %bitcast.10) | data formatting | bytes 1048576
  (1 shorter events, 0.0 us)

commit v4 on v3

--- a/solution.py
+++ b/solution.py
@@ -16,7 +16,7 @@
     na, nt, ids_ref, hidden, weight, in_t, out_f, out_ref,
     w_v, in_v, of_v, rows_v, acc, low_mine, low_recv, bc_mine, bc_recv, rs_mine, rs_recv,
     load_sem, x_ss, x_rs, core_ss, core_rs, fwd_ss, fwd_rs,
-    low_ss, low_rs, bc_ss, bc_rs, rs_ss, rs_rs, *hop,
+    low_ss, low_rs, bc_ss, bc_rs, rs_ss, rs_rs, ids_v, *hop,
 ):
     rounds, _, chunk, depth = rows_v.shape
     chips = na // 2
@@ -70,8 +70,8 @@
             barrier, inc=1, device_id=to_t(lax.rem(me_t + d, nt)),
             device_id_type=pl.DeviceIdType.MESH,
         )
-    loads[0].start()
-    loads[1].start()
+    for load in loads:
+        load.start()
     pl.semaphore_wait(barrier, na - 1 + nt - 1)
 
     def x_send(i, d):
@@ -130,8 +130,6 @@
     for d in range(1, chips):
         x_send(0, d).start()
     core_send(0).start()
-    loads[2].start()
-    loads[3].start()
 
     def front(i):
         for d in range(1, chips):
@@ -153,7 +151,7 @@
         if first:
             loads[0].wait()
             loads[1].wait()
-        ids = ids_ref[i]
+        ids = ids_v[i]
         low = jnp.zeros((rank, total), F32)
         here = rows_v[i].reshape(total, depth)
         projected = lax.dot_general(
@@ -178,7 +176,8 @@
             acc[i, :, :, cols] = part.reshape(nt, per * chunk, TILE)
             return carry
 
-        lax.fori_loop(0, width // TILE, tile, 0)
+        tiles = width // TILE
+        lax.fori_loop(0, tiles - tiles // 2, tile, 0)
         summed = low_mine[i, me_t]
         for d in range(1, nt):
             low_send(i, d).wait_recv()
@@ -186,13 +185,14 @@
         bc_mine[i] = summed.astype(BF16).astype(F32)
         for d in range(1, na):
             bc_send(i, d).start()
+        lax.fori_loop(tiles - tiles // 2, tiles, tile, 0)
 
     def back(i):
         rows_low = bc_mine[i]
         for d in range(1, na):
             bc_send(i, d).wait_recv()
             rows_low = rows_low + bc_recv[i, d]
-        ids = ids_ref[i]
+        ids = ids_v[i]
         which = lax.broadcasted_iota(jnp.int32, (every, 1, total), 0)
         spread = jnp.where(which == ids[None], rows_low[None], 0.0)
         spread = spread.reshape(every * seg, total).T.astype(BF16)
@@ -213,7 +213,7 @@
 
         @pl.when(outer)
         def _():
-            for k in range(2):
+            for k in range(1, -1, -1):
                 hop_send(i, k).start()
 
         near_send(i).start()
@@ -230,19 +230,32 @@
                 rs_mine[i, far + k] = joined.astype(BF16)
                 far_send(i, k).start()
 
+    for i in range(rounds):
+        ids_v[i] = jnp.concatenate(
+            [
+                ids_ref[:, (a * rounds + i) * chunk:(a * rounds + i + 1) * chunk]
+                for a in range(na)
+            ],
+            axis=1,
+        )
     front(0)
     middle(0, True)
+    if rounds > 1:
+        front(1)
     back(0)
 
     def body(i, carry):
-        front(i)
         middle(i, False)
+
+        @pl.when(i + 1 < rounds)
+        def _():
+            front(i + 1)
+
         relay(i - 1)
         back(i)
         return carry
 
     lax.fori_loop(1, rounds, body, 0)
-    relay(rounds - 1)
 
     def finish(i, carry):
         val = acc[i, me_t]
@@ -278,7 +291,9 @@
             bc_send(i, d).wait_send()
         return carry
 
-    lax.fori_loop(0, rounds, finish, 0)
+    lax.fori_loop(0, rounds - 1, finish, 0)
+    relay(rounds - 1)
+    finish(rounds - 1, 0)
 
 
 def shards(na, nt, hidden, weight, in_f, out_f, ids):
@@ -293,7 +308,7 @@
     total = na * chunk
     in_t = jnp.transpose(in_f, (0, 2, 1)).reshape(residents * rank, depth)
     out_f = out_f.reshape(every * seg, width)
-    ids = ids.reshape(na, rounds, chunk).transpose(1, 0, 2).reshape(rounds, 1, total)
+    ids = ids.reshape(1, na * rows_local)
     hidden = hidden.reshape(rounds, chunk, depth)
     dma = pltpu.SemaphoreType.DMA
     hop = []
@@ -329,6 +344,7 @@
             dma((rounds, nt)), dma((rounds, nt)),
             dma((rounds, na)), dma((rounds, na)),
             dma((rounds, nt)), dma((rounds, nt)),
+            pltpu.VMEM((rounds, 1, total), jnp.int32),
         ] + hop,
         compiler_params=pltpu.CompilerParams(
             collective_id=0, has_side_effects=True, vmem_limit_bytes=63 * 1024 * 1024

time: 103 us -> 95.7 us (0.929)
  Pallas kernels: 97.8 us -> 93.6 us
  other arithmetic: 1.34 us -> 0 us
  local copies, waits for them, and re-layouts: 3.15 us -> 1.88 us
    pallas_call x1, Pallas kernels: 97.8 us -> 93.6 us  [shards(): pl.pallas_call(functools.partial(kernel, na, nt), out_shape=jax.ShapeDtyp...]
    unnamed x1 -> x0, other arithmetic: 1.34 us -> none
    unnamed x2 -> x1, local copies, waits for them, and re-layouts: 2.39 us -> 1.88 us
where the time goes in v4:
time: 95.7 us; the launch traced here: 95.5 us
  Pallas kernels  93.6 us (98%)
  local copies, waits for them, and re-layouts  1.88 us (2%)
    pallas_call x1, Pallas kernels, shards(): pl.pallas_call(functools.partial(kernel, na, nt), out_shape=jax.ShapeDtyp...  93.6 us

profile of v4, /device:TPU:0, one launch (start us, length us, event | category | flops | bytes accessed | tf_op | source)
XLA Modules:
  0.0 95.5 jit_solution(10013925431888144204)
XLA Ops:
  0.0 93.6 %shard_map.55 = bf16[1,4,32,2048]{3,2,1,0:T(8,128)(2,1)} custom-call(s32[1,512]{1,0:T(1,128)} %bitcast.11, bf16[4,32,7168]{2,1,0:T(8,128)(2,1)} %bitcast.10, bf16[7168,2048]{1,0:T(8,128)(2,1)} %weight.1, bf16[512,7168]{1,0:T(8,128)(2,1)} %bitcast.8, bf16[512,2048]{1,0:T(8,128)(2,1)} %bitcast.9), custom_call_target="tpu_custom_call" | custom-call | flops 18790481920 | bytes 29360128 | tf_op jit(solution)/shard_map/pallas_call | solution.py:323
  93.6 1.9 %copy.7 = bf16[128,2048]{1,0:T(8,128)(2,1)} copy(bf16[128,2048]{1,0:T(8,128)(2,1)} %bitcast.7) | data formatting | bytes 1048576
